TPU v7x, 32 devices: a whole 2x2x4 slice. The times are simulated.
32 devices in a mesh: row: 16 (over z, y, x), rep: 2 (over core).
Axes of the slice: x: 2, y: 2, z: 4, core: 2. Of those that a mesh axis runs over, the one named last changes fastest.
Arguments:
- features: bfloat16 [8192, 256], P('row'), may hold values from -6 to 6
- weight: bfloat16 [256, 256], replicated, may hold values from -0.375 to 0.375
- bias: float32 [256], replicated, may hold values from -3 to 3
- cotangent: bfloat16 [8192, 256], P(('row', 'rep')), may hold values from -14 to 14
- tile_values: bfloat16 [16, 16, 8, 128, 128], P('row', 'rep'), may hold values from -0.125 to 0.125
- tile_index: int32 [16, 16, 8, 2], P('row', 'rep'), may hold values from 0 to 3
- tile_count: int32 [16, 16], P('row', 'rep'), may hold values from 0 to 8, as said below
- rev_values: bfloat16 [16, 16, 8, 128, 128], P('row', 'rep'), may hold values from -0.125 to 0.125
- rev_index: int32 [16, 16, 8, 2], P('row', 'rep'), may hold values from 0 to 3
- rev_count: int32 [16, 16], P('row', 'rep'), may hold values from 0 to 8, as said below
Outputs:
- activations: bfloat16 [8192, 256], P(('row', 'rep'))
- grad_features: bfloat16 [8192, 256], P(('row', 'rep'))
- grad_weight: float32 [256, 256], replicated
- grad_bias: float32 [256], replicated
Inputs may be any that keep to these rules, and one draw needn't show every extreme that they name: Slots t < tile_count[a, d] are used; some slab pair uses all 8 slots in every draw. Slots t < rev_count[a, d] are used; some slab pair uses all 8 slots in every draw.
All inputs are finite; a program needn't handle non-finite values.
Results may differ from a plain program's by a relative error of at most 0.006.
Values may be sent and summed in bfloat16 or wider, within the bound.
A program may use at most 64 MiB of HBM per device.

v0:
```python
import jax
import jax.numpy as jnp
from jax import lax
from jax.sharding import PartitionSpec as P

TILE = 128
BLOCKS = 4


def passed_along(value, axis, steps):
    count = lax.axis_size(axis)
    pairs = [(source, (source + steps) % count) for source in range(count)]
    return lax.ppermute(value, axis, pairs)


def section_term(current, tile_block, slot_index, counts):
    blocks = current.reshape(BLOCKS, TILE, current.shape[1])
    sources = jnp.take(blocks, slot_index[:, 1], axis=0)
    product = jnp.einsum("tab,tbf->taf", tile_block, sources, preferred_element_type=jnp.float32)
    usable = jnp.arange(slot_index.shape[0], dtype=jnp.int32) < counts
    placing = (
        (slot_index[:, 0][None, :] == jnp.arange(BLOCKS, dtype=jnp.int32)[:, None])
        & usable[None, :]
    ).astype(jnp.float32)
    return jnp.einsum("nt,taf->naf", placing, product, precision=lax.Precision.HIGHEST)


def first_source(source, sections):
    rep_index = lax.axis_index("rep")
    groups = lax.axis_size("rep")
    current = source
    for shift_bit in range(groups.bit_length() - 1):
        shifted = passed_along(current, "row", -(sections << shift_bit))
        current = jnp.where(rep_index >> shift_bit & 1 == 1, shifted, current)
    return current


def apply_tiles(source, values, slot_index, counts):
    sections = values.shape[1]
    current = first_source(source, sections)
    summed_rows = jnp.zeros((BLOCKS, TILE, source.shape[1]), jnp.float32)
    for section in range(sections):
        if section > 0:
            current = passed_along(current, "row", -1)
        summed_rows = summed_rows + section_term(
            current, values[0, section], slot_index[0, section], counts[0, section]
        )
    return summed_rows.reshape(source.shape[0], source.shape[1])


def reduce_part(partial_rows):
    return lax.psum(partial_rows, "rep")


def own_rows(matrix):
    share_size = matrix.shape[0] // lax.axis_size("rep")
    return lax.dynamic_slice_in_dim(matrix, lax.axis_index("rep") * share_size, share_size, 0)


def activate(preact, cotangent):
    sigmoid_pre = jax.nn.sigmoid(preact)
    activations = (preact * sigmoid_pre).astype(jnp.bfloat16)
    grad_pre = (
        cotangent.astype(jnp.float32) * sigmoid_pre * (1.0 + preact * (1.0 - sigmoid_pre))
    ).astype(jnp.bfloat16)
    return (activations, grad_pre)


def local(
    features,
    weight,
    bias,
    cotangent,
    tile_values,
    tile_index,
    tile_count,
    rev_values,
    rev_index,
    rev_count,
):
    node_total = features.shape[0] * lax.axis_size("row")
    grad_scale = float(node_total) ** (-0.5)
    summed = reduce_part(apply_tiles(features, tile_values, tile_index, tile_count))
    mixed_all = summed.astype(jnp.bfloat16)
    preact_all = jnp.dot(mixed_all, weight, preferred_element_type=jnp.float32) + bias
    cotangent_all = lax.all_gather(cotangent, "rep", axis=0, tiled=True)
    activ_all, grad_all = activate(preact_all, cotangent_all)
    image = jnp.einsum("ng,fg->nf", grad_all, weight, preferred_element_type=jnp.float32).astype(
        jnp.bfloat16
    )
    mixed_rows = own_rows(mixed_all)
    grad_pre = own_rows(grad_all)
    activations = own_rows(activ_all)
    weight_term = jnp.einsum("nf,ng->fg", mixed_rows, grad_pre, preferred_element_type=jnp.float32)
    bias_term = jnp.sum(grad_pre.astype(jnp.float32), axis=0)
    grad_weight, grad_bias = lax.psum((weight_term, bias_term), ("row", "rep"))
    back_rows = reduce_part(apply_tiles(image, rev_values, rev_index, rev_count))
    back_rows = own_rows(back_rows)
    return (
        activations,
        back_rows.astype(jnp.bfloat16),
        grad_weight * grad_scale,
        grad_bias * grad_scale,
    )


def solution(mesh):
    placed = (
        P("row", None),
        P(),
        P(),
        P(("row", "rep"), None),
        P("row", "rep", None, None, None),
        P("row", "rep", None, None),
        P("row", "rep"),
        P("row", "rep", None, None, None),
        P("row", "rep", None, None),
        P("row", "rep"),
    )
    return jax.shard_map(
        local,
        mesh=mesh,
        in_specs=placed,
        out_specs=(P(("row", "rep"), None), P(("row", "rep"), None), P(), P()),
        check_vma=False,
    )
```

profile of v0, /device:TPU:0, one launch (start us, length us, event | category | flops | bytes accessed | tf_op | source)
XLA Modules:
  0.0 381.1 jit_solution(8210804947538525664)
XLA Ops:
  7.2 4.1 %collective-permute-start = (bf16[512,256]{1,0:T(8,128)(2,1)}, bf16[512,256]{1,0:T(8,128)(2,1)S(1)}, u32[]{:S(2)}, u32[]{:S(2)}) collective-permute-start(bf16[512,256]{1,0:T(8,128)(2,1)} %param.12), channel_id=1, source_target_pairs={{0,16},{2,18},{4,20},{6,22},{8,24},{10,26},{12,28},{14,30},{16,0},... | collective-permute-start | bytes 786440 | tf_op jit(solution)/shard_map/ppermute | solution.py:13
  23.6 1.6 fusion.216
  38.3 1.6 fusion.215
  52.1 3.5 all_gather.3
  57.3 3.3 collective-permute-start.1
  63.6 2.1 collective-permute-done.1
  68.1 6.1 %collective-permute-start.2 = (bf16[512,256]{1,0:T(8,128)(2,1)S(1)}, bf16[512,256]{1,0:T(8,128)(2,1)S(1)}, u32[]{:S(2)}, u32[]{:S(2)}) collective-permute-start(bf16[512,256]{1,0:T(8,128)(2,1)S(1)} %collective-permute-done.1), channel_id=1, source_target_pairs={{0,30},{2,0},{4,2},{6,4},{8,6},{10,8},{12,10},{14,12},{16,14},{18,... | collective-permute-start | bytes 786440 | tf_op jit(solution)/shard_map/ppermute | solution.py:13
  75.6 2.9 collective-permute-done.2
  79.2 1.4 fusion.44
  81.1 6.1 %collective-permute-start.3 = (bf16[512,256]{1,0:T(8,128)(2,1)S(1)}, bf16[512,256]{1,0:T(8,128)(2,1)S(1)}, u32[]{:S(2)}, u32[]{:S(2)}) collective-permute-start(bf16[512,256]{1,0:T(8,128)(2,1)S(1)} %copy-done.2), channel_id=1, source_target_pairs={{0,30},{2,0},{4,2},{6,4},{8,6},{10,8},{12,10},{14,12},{16,14},{18,... | collective-permute-start | bytes 786440 | tf_op jit(solution)/shard_map/ppermute | solution.py:13
  88.5 2.6 collective-permute-done.3
  91.9 1.4 fusion.42
  93.8 6.1 %collective-permute-start.4 = (bf16[512,256]{1,0:T(8,128)(2,1)S(1)}, bf16[512,256]{1,0:T(8,128)(2,1)S(1)}, u32[]{:S(2)}, u32[]{:S(2)}) collective-permute-start(bf16[512,256]{1,0:T(8,128)(2,1)S(1)} %copy-done.4), channel_id=1, source_target_pairs={{0,30},{2,0},{4,2},{6,4},{8,6},{10,8},{12,10},{14,12},{16,14},{18,... | collective-permute-start | bytes 786440 | tf_op jit(solution)/shard_map/ppermute | solution.py:13
  101.2 2.6 collective-permute-done.4
  104.6 1.4 fusion.40
  106.5 6.1 %collective-permute-start.5 = (bf16[512,256]{1,0:T(8,128)(2,1)S(1)}, bf16[512,256]{1,0:T(8,128)(2,1)S(1)}, u32[]{:S(2)}, u32[]{:S(2)}) collective-permute-start(bf16[512,256]{1,0:T(8,128)(2,1)S(1)} %copy-done.6), channel_id=1, source_target_pairs={{0,30},{2,0},{4,2},{6,4},{8,6},{10,8},{12,10},{14,12},{16,14},{18,... | collective-permute-start | bytes 786440 | tf_op jit(solution)/shard_map/ppermute | solution.py:13
  113.9 2.6 collective-permute-done.5
  117.2 1.4 fusion.38
  119.1 6.1 %collective-permute-start.6 = (bf16[512,256]{1,0:T(8,128)(2,1)S(1)}, bf16[512,256]{1,0:T(8,128)(2,1)S(1)}, u32[]{:S(2)}, u32[]{:S(2)}) collective-permute-start(bf16[512,256]{1,0:T(8,128)(2,1)S(1)} %copy-done.8), channel_id=1, source_target_pairs={{0,30},{2,0},{4,2},{6,4},{8,6},{10,8},{12,10},{14,12},{16,14},{18,... | collective-permute-start | bytes 786440 | tf_op jit(solution)/shard_map/ppermute | solution.py:13
  126.6 2.6 collective-permute-done.6
  129.9 1.4 fusion.36
  131.8 6.3 %collective-permute-start.7 = (bf16[512,256]{1,0:T(8,128)(2,1)S(1)}, bf16[512,256]{1,0:T(8,128)(2,1)S(1)}, u32[]{:S(2)}, u32[]{:S(2)}) collective-permute-start(bf16[512,256]{1,0:T(8,128)(2,1)S(1)} %copy-done.10), channel_id=1, source_target_pairs={{0,30},{2,0},{4,2},{6,4},{8,6},{10,8},{12,10},{14,12},{16,14},{18,... | collective-permute-start | bytes 786440 | tf_op jit(solution)/shard_map/ppermute | solution.py:13
  139.4 2.6 collective-permute-done.7
  142.7 1.4 fusion.34
  145.4 4.8 %all-reduce.5 = bf16[512,256]{1,0:T(8,128)(2,1)S(1)} all-reduce(f32[512,256]{1,0:T(8,128)S(1)} %bitcast.296), channel_id=1, replica_groups=mesh['row'=16,'rep'=2] {'rep'}, use_global_device_ids=true, to_apply=%region_0.2 | all-reduce | flops 131072 | bytes 786432 | tf_op jit(solution)/shard_map/psum | solution.py:52
  152.0 43.5 %psum.31 = f32[256]{0:T(256)S(1)} all-reduce(f32[256]{0:T(256)S(1)} %convert_reduce_fusion), channel_id=1, replica_groups=mesh['row'=16,'rep'=2] {'row','rep'}, use_global_device_ids=true, to_apply=%region_4.6 | all-reduce | flops 256 | bytes 2048 | tf_op jit(solution)/shard_map/psum | solution.py:96
  196.7 82.9 %all-reduce.4.cloned.1.call-done = f32[256,256]{1,0:T(8,128)} async-done(((f32[256,256]{1,0:T(8,128)}), f32[256,256]{1,0:T(8,128)}) %all-reduce.4.cloned.1.call-update) | async-done | bytes 262160 | tf_op jit(solution)/shard_map/psum | solution.py:96
  279.6 1.7 broadcast_multiply_fusion
  281.3 3.3 collective-permute-start.9
  287.9 1.5 collective-permute-done.9
  292.0 6.1 %collective-permute-start.10 = (bf16[512,256]{1,0:T(8,128)(2,1)S(1)}, bf16[512,256]{1,0:T(8,128)(2,1)S(1)}, u32[]{:S(2)}, u32[]{:S(2)}) collective-permute-start(bf16[512,256]{1,0:T(8,128)(2,1)S(1)} %collective-permute-done.9), channel_id=1, source_target_pairs={{0,30},{2,0},{4,2},{6,4},{8,6},{10,8},{12,10},{14,12},{16,14},{18,... | collective-permute-start | bytes 786440 | tf_op jit(solution)/shard_map/ppermute | solution.py:13
  299.4 2.6 collective-permute-done.10
  302.7 1.4 fusion.28
  304.7 6.1 %collective-permute-start.11 = (bf16[512,256]{1,0:T(8,128)(2,1)S(1)}, bf16[512,256]{1,0:T(8,128)(2,1)S(1)}, u32[]{:S(2)}, u32[]{:S(2)}) collective-permute-start(bf16[512,256]{1,0:T(8,128)(2,1)S(1)} %copy-done.12), channel_id=1, source_target_pairs={{0,30},{2,0},{4,2},{6,4},{8,6},{10,8},{12,10},{14,12},{16,14},{18,... | collective-permute-start | bytes 786440 | tf_op jit(solution)/shard_map/ppermute | solution.py:13
  312.1 2.6 collective-permute-done.11
  315.4 1.4 fusion.26
  317.3 6.1 %collective-permute-start.12 = (bf16[512,256]{1,0:T(8,128)(2,1)S(1)}, bf16[512,256]{1,0:T(8,128)(2,1)S(1)}, u32[]{:S(2)}, u32[]{:S(2)}) collective-permute-start(bf16[512,256]{1,0:T(8,128)(2,1)S(1)} %copy-done.14), channel_id=1, source_target_pairs={{0,30},{2,0},{4,2},{6,4},{8,6},{10,8},{12,10},{14,12},{16,14},{18,... | collective-permute-start | bytes 786440 | tf_op jit(solution)/shard_map/ppermute | solution.py:13
  324.7 2.6 collective-permute-done.12
  328.1 1.4 fusion.24
  330.0 6.4 %collective-permute-start.13 = (bf16[512,256]{1,0:T(8,128)(2,1)S(1)}, bf16[512,256]{1,0:T(8,128)(2,1)S(1)}, u32[]{:S(2)}, u32[]{:S(2)}) collective-permute-start(bf16[512,256]{1,0:T(8,128)(2,1)S(1)} %copy-done.16), channel_id=1, source_target_pairs={{0,30},{2,0},{4,2},{6,4},{8,6},{10,8},{12,10},{14,12},{16,14},{18,... | collective-permute-start | bytes 786440 | tf_op jit(solution)/shard_map/ppermute | solution.py:13
  337.5 2.7 collective-permute-done.13
  340.9 1.4 fusion.22
  342.8 6.1 %collective-permute-start.14 = (bf16[512,256]{1,0:T(8,128)(2,1)S(1)}, bf16[512,256]{1,0:T(8,128)(2,1)S(1)}, u32[]{:S(2)}, u32[]{:S(2)}) collective-permute-start(bf16[512,256]{1,0:T(8,128)(2,1)S(1)} %copy-done.18), channel_id=1, source_target_pairs={{0,30},{2,0},{4,2},{6,4},{8,6},{10,8},{12,10},{14,12},{16,14},{18,... | collective-permute-start | bytes 786440 | tf_op jit(solution)/shard_map/ppermute | solution.py:13
  349.6 3.3 collective-permute-done.14
  353.6 1.4 fusion.20
  355.5 6.1 %collective-permute-start.15 = (bf16[512,256]{1,0:T(8,128)(2,1)S(1)}, bf16[512,256]{1,0:T(8,128)(2,1)S(1)}, u32[]{:S(2)}, u32[]{:S(2)}) collective-permute-start(bf16[512,256]{1,0:T(8,128)(2,1)S(1)} %copy-done.20), channel_id=1, source_target_pairs={{0,30},{2,0},{4,2},{6,4},{8,6},{10,8},{12,10},{14,12},{16,14},{18,... | collective-permute-start | bytes 786440 | tf_op jit(solution)/shard_map/ppermute | solution.py:13
  362.3 3.3 collective-permute-done.15
  368.7 4.8 %all-reduce.6 = bf16[512,256]{1,0:T(8,128)(2,1)S(1)} all-reduce(f32[512,256]{1,0:T(8,128)S(1)} %bitcast.297), channel_id=1, replica_groups=mesh['row'=16,'rep'=2] {'rep'}, use_global_device_ids=true, to_apply=%region_1.3 | all-reduce | flops 131072 | bytes 786432 | tf_op jit(solution)/shard_map/psum | solution.py:52
  (201 shorter events, 84.8 us)
Async XLA Ops:
  7.2 143.1 %copy-start = (bf16[256,256]{1,0:T(8,128)(2,1)S(1)}, bf16[256,256]{1,0:T(8,128)(2,1)}, u32[]{:S(2)}) copy-start(bf16[256,256]{1,0:T(8,128)(2,1)} %param.13) | copy-start | bytes 393220
  7.2 272.4 %all-reduce.4.cloned.1.call-start = ((), (), s32[]{:S(2)}) async-start(), calls=%async_computation | async-start | bytes 524288 | tf_op jit(solution)/shard_map/psum | solution.py:96
  7.2 49.0 %collective-permute-start = (bf16[512,256]{1,0:T(8,128)(2,1)}, bf16[512,256]{1,0:T(8,128)(2,1)S(1)}, u32[]{:S(2)}, u32[]{:S(2)}) collective-permute-start(bf16[512,256]{1,0:T(8,128)(2,1)} %param.12), channel_id=1, source_target_pairs={{0,16},{2,18},{4,20},{6,22},{8,24},{10,26},{12,28},{14,30},{16,0},... | collective-permute-start | bytes 786440 | tf_op jit(solution)/shard_map/ppermute | solution.py:13
  57.3 8.4 %collective-permute-start.1 = (bf16[512,256]{1,0:T(8,128)(2,1)S(1)}, bf16[512,256]{1,0:T(8,128)(2,1)S(1)}, u32[]{:S(2)}, u32[]{:S(2)}) collective-permute-start(bf16[512,256]{1,0:T(8,128)(2,1)S(1)} %broadcast_select_fusion.1), channel_id=1, source_target_pairs={{0,30},{2,0},{4,2},{6,4},{8,6},{10,8},{12,10},{14,12},{16,14},{18,... | collective-permute-start | bytes 786440 | tf_op jit(solution)/shard_map/ppermute | solution.py:13
  68.1 10.4 %collective-permute-start.2 = (bf16[512,256]{1,0:T(8,128)(2,1)S(1)}, bf16[512,256]{1,0:T(8,128)(2,1)S(1)}, u32[]{:S(2)}, u32[]{:S(2)}) collective-permute-start(bf16[512,256]{1,0:T(8,128)(2,1)S(1)} %collective-permute-done.1), channel_id=1, source_target_pairs={{0,30},{2,0},{4,2},{6,4},{8,6},{10,8},{12,10},{14,12},{16,14},{18,... | collective-permute-start | bytes 786440 | tf_op jit(solution)/shard_map/ppermute | solution.py:13
  79.2 1.9 copy-start.2
  81.1 10.0 %collective-permute-start.3 = (bf16[512,256]{1,0:T(8,128)(2,1)S(1)}, bf16[512,256]{1,0:T(8,128)(2,1)S(1)}, u32[]{:S(2)}, u32[]{:S(2)}) collective-permute-start(bf16[512,256]{1,0:T(8,128)(2,1)S(1)} %copy-done.2), channel_id=1, source_target_pairs={{0,30},{2,0},{4,2},{6,4},{8,6},{10,8},{12,10},{14,12},{16,14},{18,... | collective-permute-start | bytes 786440 | tf_op jit(solution)/shard_map/ppermute | solution.py:13
  91.9 1.9 copy-start.4
  93.8 10.0 %collective-permute-start.4 = (bf16[512,256]{1,0:T(8,128)(2,1)S(1)}, bf16[512,256]{1,0:T(8,128)(2,1)S(1)}, u32[]{:S(2)}, u32[]{:S(2)}) collective-permute-start(bf16[512,256]{1,0:T(8,128)(2,1)S(1)} %copy-done.4), channel_id=1, source_target_pairs={{0,30},{2,0},{4,2},{6,4},{8,6},{10,8},{12,10},{14,12},{16,14},{18,... | collective-permute-start | bytes 786440 | tf_op jit(solution)/shard_map/ppermute | solution.py:13
  103.8 0.7 copy-start.5
  104.5 1.9 copy-start.6
  106.5 10.0 %collective-permute-start.5 = (bf16[512,256]{1,0:T(8,128)(2,1)S(1)}, bf16[512,256]{1,0:T(8,128)(2,1)S(1)}, u32[]{:S(2)}, u32[]{:S(2)}) collective-permute-start(bf16[512,256]{1,0:T(8,128)(2,1)S(1)} %copy-done.6), channel_id=1, source_target_pairs={{0,30},{2,0},{4,2},{6,4},{8,6},{10,8},{12,10},{14,12},{16,14},{18,... | collective-permute-start | bytes 786440 | tf_op jit(solution)/shard_map/ppermute | solution.py:13
  116.5 0.7 copy-start.7
  117.2 1.9 copy-start.8
  119.1 10.0 %collective-permute-start.6 = (bf16[512,256]{1,0:T(8,128)(2,1)S(1)}, bf16[512,256]{1,0:T(8,128)(2,1)S(1)}, u32[]{:S(2)}, u32[]{:S(2)}) collective-permute-start(bf16[512,256]{1,0:T(8,128)(2,1)S(1)} %copy-done.8), channel_id=1, source_target_pairs={{0,30},{2,0},{4,2},{6,4},{8,6},{10,8},{12,10},{14,12},{16,14},{18,... | collective-permute-start | bytes 786440 | tf_op jit(solution)/shard_map/ppermute | solution.py:13
  129.2 0.7 copy-start.9
  129.9 1.9 copy-start.10
  131.8 10.2 %collective-permute-start.7 = (bf16[512,256]{1,0:T(8,128)(2,1)S(1)}, bf16[512,256]{1,0:T(8,128)(2,1)S(1)}, u32[]{:S(2)}, u32[]{:S(2)}) collective-permute-start(bf16[512,256]{1,0:T(8,128)(2,1)S(1)} %copy-done.10), channel_id=1, source_target_pairs={{0,30},{2,0},{4,2},{6,4},{8,6},{10,8},{12,10},{14,12},{16,14},{18,... | collective-permute-start | bytes 786440 | tf_op jit(solution)/shard_map/ppermute | solution.py:13
  142.7 1.9 copy-start.27
  142.7 1.9 copy-start.35
  144.6 5.6 %copy-start.21 = (bf16[512,256]{1,0:T(8,128)(2,1)S(1)}, bf16[512,256]{1,0:T(8,128)(2,1)}, u32[]{:S(2)}) copy-start(bf16[512,256]{1,0:T(8,128)(2,1)} %all_gather.3) | copy-start | bytes 786436
  144.6 5.6 %copy-start.36 = (f32[256]{0:T(256)S(1)}, f32[256]{0:T(256)}, u32[]{:S(2)}) copy-start(f32[256]{0:T(256)} %param.14) | copy-start | bytes 3076
  150.9 134.5 %copy-start.33 = (pred[8]{0:T(512)(128)(4,1)S(1)}, pred[8]{0:T(512)(128)(4,1)}, u32[]{:S(2)}) copy-start(pred[8]{0:T(512)(128)(4,1)} %get-tuple-element.19) | copy-start | bytes 28
  151.9 129.4 %collective-permute-start.8 = (bf16[512,256]{1,0:T(8,128)(2,1)S(1)}, bf16[512,256]{1,0:T(8,128)(2,1)S(1)}, u32[]{:S(2)}, u32[]{:S(2)}) collective-permute-start(bf16[512,256]{1,0:T(8,128)(2,1)S(1)} %convolution_convert_fusion), channel_id=1, source_target_pairs={{0,16},{2,18},{4,20},{6,22},{8,24},{10,26},{12,28},{14,30},{16,0},... | collective-permute-start | bytes 786440 | tf_op jit(solution)/shard_map/ppermute | solution.py:13
  281.3 8.1 %collective-permute-start.9 = (bf16[512,256]{1,0:T(8,128)(2,1)S(1)}, bf16[512,256]{1,0:T(8,128)(2,1)S(1)}, u32[]{:S(2)}, u32[]{:S(2)}) collective-permute-start(bf16[512,256]{1,0:T(8,128)(2,1)S(1)} %broadcast_select_fusion), channel_id=1, source_target_pairs={{0,30},{2,0},{4,2},{6,4},{8,6},{10,8},{12,10},{14,12},{16,14},{18,... | collective-permute-start | bytes 786440 | tf_op jit(solution)/shard_map/ppermute | solution.py:13
  285.3 1.9 copy-start.22
  285.3 1.9 copy-start.28
  286.7 3.4 copy-start.31
  292.0 10.0 %collective-permute-start.10 = (bf16[512,256]{1,0:T(8,128)(2,1)S(1)}, bf16[512,256]{1,0:T(8,128)(2,1)S(1)}, u32[]{:S(2)}, u32[]{:S(2)}) collective-permute-start(bf16[512,256]{1,0:T(8,128)(2,1)S(1)} %collective-permute-done.9), channel_id=1, source_target_pairs={{0,30},{2,0},{4,2},{6,4},{8,6},{10,8},{12,10},{14,12},{16,14},{18,... | collective-permute-start | bytes 786440 | tf_op jit(solution)/shard_map/ppermute | solution.py:13
  302.0 0.7 copy-start.11
  302.7 1.9 copy-start.12
  304.7 10.0 %collective-permute-start.11 = (bf16[512,256]{1,0:T(8,128)(2,1)S(1)}, bf16[512,256]{1,0:T(8,128)(2,1)S(1)}, u32[]{:S(2)}, u32[]{:S(2)}) collective-permute-start(bf16[512,256]{1,0:T(8,128)(2,1)S(1)} %copy-done.12), channel_id=1, source_target_pairs={{0,30},{2,0},{4,2},{6,4},{8,6},{10,8},{12,10},{14,12},{16,14},{18,... | collective-permute-start | bytes 786440 | tf_op jit(solution)/shard_map/ppermute | solution.py:13
  315.4 1.9 copy-start.14
  317.3 10.0 %collective-permute-start.12 = (bf16[512,256]{1,0:T(8,128)(2,1)S(1)}, bf16[512,256]{1,0:T(8,128)(2,1)S(1)}, u32[]{:S(2)}, u32[]{:S(2)}) collective-permute-start(bf16[512,256]{1,0:T(8,128)(2,1)S(1)} %copy-done.14), channel_id=1, source_target_pairs={{0,30},{2,0},{4,2},{6,4},{8,6},{10,8},{12,10},{14,12},{16,14},{18,... | collective-permute-start | bytes 786440 | tf_op jit(solution)/shard_map/ppermute | solution.py:13
  328.1 8.3 %copy-start.24 = (s32[8]{0:T(128)S(1)}, s32[8]{0:T(128)}, u32[]{:S(2)}) copy-start(s32[8]{0:T(128)} %get-tuple-element.83) | copy-start | bytes 100
  328.1 1.9 copy-start.16
  330.0 10.2 %collective-permute-start.13 = (bf16[512,256]{1,0:T(8,128)(2,1)S(1)}, bf16[512,256]{1,0:T(8,128)(2,1)S(1)}, u32[]{:S(2)}, u32[]{:S(2)}) collective-permute-start(bf16[512,256]{1,0:T(8,128)(2,1)S(1)} %copy-done.16), channel_id=1, source_target_pairs={{0,30},{2,0},{4,2},{6,4},{8,6},{10,8},{12,10},{14,12},{16,14},{18,... | collective-permute-start | bytes 786440 | tf_op jit(solution)/shard_map/ppermute | solution.py:13
  340.9 8.1 %copy-start.23 = (s32[8]{0:T(128)S(1)}, s32[8]{0:T(128)}, u32[]{:S(2)}) copy-start(s32[8]{0:T(128)} %get-tuple-element.82) | copy-start | bytes 100
  340.9 8.1 %copy-start.34 = (pred[8]{0:T(512)(128)(4,1)S(1)}, pred[8]{0:T(512)(128)(4,1)}, u32[]{:S(2)}) copy-start(pred[8]{0:T(512)(128)(4,1)} %iota_compare_fusion.18) | copy-start | bytes 28
  340.9 1.9 copy-start.18
  342.8 10.0 %collective-permute-start.14 = (bf16[512,256]{1,0:T(8,128)(2,1)S(1)}, bf16[512,256]{1,0:T(8,128)(2,1)S(1)}, u32[]{:S(2)}, u32[]{:S(2)}) collective-permute-start(bf16[512,256]{1,0:T(8,128)(2,1)S(1)} %copy-done.18), channel_id=1, source_target_pairs={{0,30},{2,0},{4,2},{6,4},{8,6},{10,8},{12,10},{14,12},{16,14},{18,... | collective-permute-start | bytes 786440 | tf_op jit(solution)/shard_map/ppermute | solution.py:13
  353.6 8.1 %copy-start.26 = (s32[8]{0:T(128)S(1)}, s32[8]{0:T(128)}, u32[]{:S(2)}) copy-start(s32[8]{0:T(128)} %get-tuple-element.81) | copy-start | bytes 100
  353.6 8.1 %copy-start.32 = (pred[8]{0:T(512)(128)(4,1)S(1)}, pred[8]{0:T(512)(128)(4,1)}, u32[]{:S(2)}) copy-start(pred[8]{0:T(512)(128)(4,1)} %iota_compare_fusion.17) | copy-start | bytes 28
  353.6 1.9 copy-start.20
  355.5 10.6 %copy-start.30 = (pred[8]{0:T(512)(128)(4,1)S(1)}, pred[8]{0:T(512)(128)(4,1)}, u32[]{:S(2)}) copy-start(pred[8]{0:T(512)(128)(4,1)} %get-tuple-element.5) | copy-start | bytes 28
  355.5 10.0 %collective-permute-start.15 = (bf16[512,256]{1,0:T(8,128)(2,1)S(1)}, bf16[512,256]{1,0:T(8,128)(2,1)S(1)}, u32[]{:S(2)}, u32[]{:S(2)}) collective-permute-start(bf16[512,256]{1,0:T(8,128)(2,1)S(1)} %copy-done.20), channel_id=1, source_target_pairs={{0,30},{2,0},{4,2},{6,4},{8,6},{10,8},{12,10},{14,12},{16,14},{18,... | collective-permute-start | bytes 786440 | tf_op jit(solution)/shard_map/ppermute | solution.py:13
  366.1 1.9 copy-start.25
  366.1 1.9 copy-start.29
  (6 other events, 4.3 us)
Sparse Core Ops, SparseCore 0:
  152.1 127.4 all-reduce.3
where the time goes:
time: 382 us; the launch traced here: 381 us
  waiting for transfers between devices  119 us (31%)
  starting transfers between devices  84.8 us (22%)
  blocking collectives  56.7 us (15%)
  matrix products  40.4 us (11%)
  other arithmetic  35.9 us (9%)
  local copies, waits for them, and re-layouts  28.9 us (8%)
  between operations  15 us (4%)
    ppermute x16, starting transfers between devices, passed_along(): return lax.ppermute(value, axis, pairs)  84.7 us
    psum x1, waiting for transfers between devices, local(): grad_weight, grad_bias = lax.psum((weight_term, bias_term), ('row', 'rep'))  82.9 us
    psum x1, blocking collectives, local(): grad_weight, grad_bias = lax.psum((weight_term, bias_term), ('row', 'rep'))  43.5 us
    ppermute x16, waiting for transfers between devices, passed_along(): return lax.ppermute(value, axis, pairs)  36.6 us
    dot_general x16, matrix products, section_term(): jnp.einsum('tab,tbf->taf', tile_block, sources, preferred_element_type=jn...  22.4 us
    lt x16, other arithmetic, section_term(): usable = jnp.arange(slot_index.shape[0], dtype=jnp.int32) < counts  18.2 us
    dot_general x16, matrix products, section_term(): jnp.einsum('nt,taf->naf', placing, product, precision=lax.Precision.HIGHEST)  16.4 us
    gather x16, local copies, waits for them, and re-layouts, section_term(): sources = jnp.take(blocks, slot_index[:, 1], axis=0)  10.5 us
  transfers between devices with their start and end apart: 17, of which 15 were waited for; matrix products, arithmetic and copies ran while one was open for 17% of the time, Pallas kernels for 0%

commit v1 on v0

--- a/solution.py
+++ b/solution.py
@@ -49,7 +49,11 @@
 
 
 def reduce_part(partial_rows):
-    return lax.psum(partial_rows, "rep")
+
+    def sectors_see(local_block, mesh_name):
+        return lax.all_gather(local_block, mesh_name).sum(axis=0)
+
+    return sectors_see(partial_rows, mesh_name="rep")
 
 
 def own_rows(matrix):

time: 382 us -> 321 us (0.84)
  waiting for transfers between devices: 119 us -> 57.7 us
  blocking collectives: 56.7 us -> 42.5 us
  local copies, waits for them, and re-layouts: 28.9 us -> 35.8 us
  starting transfers between devices: 84.8 us -> 90.1 us
    psum x1, waiting for transfers between devices: 82.9 us -> 0.01 us  [local(): grad_weight, grad_bias = lax.psum((weight_term, bias_term), ('row', 'rep'))]
    ppermute x16, waiting for transfers between devices: 36.6 us -> 51.6 us  [passed_along(): return lax.ppermute(value, axis, pairs)]
    psum x2 -> x0, blocking collectives: 9.65 us -> none  [reduce_part(): return lax.psum(partial_rows, 'rep')]
    all_gather x0 -> x2, waiting for transfers between devices: none -> 6.11 us  [sectors_see(): return lax.all_gather(local_block, mesh_name).sum(axis=0)]
    gather x16, local copies, waits for them, and re-layouts: 10.5 us -> 16.2 us  [section_term(): sources = jnp.take(blocks, slot_index[:, 1], axis=0)]
    ppermute x16, starting transfers between devices: 84.7 us -> 90 us  [passed_along(): return lax.ppermute(value, axis, pairs)]
  transfers between devices with their start and end apart: 17 -> 19, of which waited for: 15 -> 16; matrix products, arithmetic and copies ran while one was open for 17% -> 28% of each run, Pallas kernels for 0% -> 0%
where the time goes in v1:
time: 321 us; the launch traced here: 320 us
  starting transfers between devices  90.1 us (28%)
  waiting for transfers between devices  57.7 us (18%)
  blocking collectives  42.5 us (13%)
  matrix products  39.7 us (12%)
  other arithmetic  39.2 us (12%)
  local copies, waits for them, and re-layouts  35.8 us (11%)
  between operations  14.9 us (5%)
    ppermute x16, starting transfers between devices, passed_along(): return lax.ppermute(value, axis, pairs)  90 us
    ppermute x16, waiting for transfers between devices, passed_along(): return lax.ppermute(value, axis, pairs)  51.6 us
    psum x1, blocking collectives, local(): grad_weight, grad_bias = lax.psum((weight_term, bias_term), ('row', 'rep'))  40.5 us
    dot_general x16, matrix products, section_term(): jnp.einsum('tab,tbf->taf', tile_block, sources, preferred_element_type=jn...  22.2 us
    lt x16, other arithmetic, section_term(): usable = jnp.arange(slot_index.shape[0], dtype=jnp.int32) < counts  18.2 us
    gather x16, local copies, waits for them, and re-layouts, section_term(): sources = jnp.take(blocks, slot_index[:, 1], axis=0)  16.2 us
    dot_general x16, matrix products, section_term(): jnp.einsum('nt,taf->naf', placing, product, precision=lax.Precision.HIGHEST)  15 us
    and x16, other arithmetic, section_term(): sources = jnp.take(blocks, slot_index[:, 1], axis=0)  8.41 us
  transfers between devices with their start and end apart: 19, of which 16 were waited for; matrix products, arithmetic and copies ran while one was open for 28% of the time, Pallas kernels for 0%

profile of v1, /device:TPU:0, one launch (start us, length us, event | category | flops | bytes accessed | tf_op | source)
XLA Modules:
  0.0 320.0 jit_solution(944693474219179211)
XLA Ops:
  7.2 4.1 %collective-permute-start = (bf16[512,256]{1,0:T(8,128)(2,1)}, bf16[512,256]{1,0:T(8,128)(2,1)S(1)}, u32[]{:S(2)}, u32[]{:S(2)}) collective-permute-start(bf16[512,256]{1,0:T(8,128)(2,1)} %param.12), channel_id=1, source_target_pairs={{0,16},{2,18},{4,20},{6,22},{8,24},{10,26},{12,28},{14,30},{16,0},... | collective-permute-start | bytes 786440 | tf_op jit(solution)/shard_map/ppermute | solution.py:13
  16.5 1.6 fusion.184
  33.7 1.6 fusion.183
  49.8 3.3 %collective-permute-start.1 = (bf16[512,256]{1,0:T(8,128)(2,1)S(1)}, bf16[512,256]{1,0:T(8,128)(2,1)S(1)}, u32[]{:S(2)}, u32[]{:S(2)}) collective-permute-start(bf16[512,256]{1,0:T(8,128)(2,1)S(1)} %broadcast_select_fusion.1), channel_id=1, source_target_pairs={{0,30},{2,0},{4,2},{6,4},{8,6},{10,8},{12,10},{14,12},{16,14},{18,... | collective-permute-start | bytes 786440 | tf_op jit(solution)/shard_map/ppermute | solution.py:13
  59.9 6.1 %collective-permute-start.2 = (bf16[512,256]{1,0:T(8,128)(2,1)S(1)}, bf16[512,256]{1,0:T(8,128)(2,1)S(1)}, u32[]{:S(2)}, u32[]{:S(2)}) collective-permute-start(bf16[512,256]{1,0:T(8,128)(2,1)S(1)} %collective-permute-done.1), channel_id=1, source_target_pairs={{0,30},{2,0},{4,2},{6,4},{8,6},{10,8},{12,10},{14,12},{16,14},{18,... | collective-permute-start | bytes 786440 | tf_op jit(solution)/shard_map/ppermute | solution.py:13
  67.3 2.6 collective-permute-done.2
  70.6 1.4 convolution_bitcast_fusion.13
  72.5 6.1 %collective-permute-start.3 = (bf16[512,256]{1,0:T(8,128)(2,1)S(1)}, bf16[512,256]{1,0:T(8,128)(2,1)S(1)}, u32[]{:S(2)}, u32[]{:S(2)}) collective-permute-start(bf16[512,256]{1,0:T(8,128)(2,1)S(1)} %copy-done.2), channel_id=1, source_target_pairs={{0,30},{2,0},{4,2},{6,4},{8,6},{10,8},{12,10},{14,12},{16,14},{18,... | collective-permute-start | bytes 786440 | tf_op jit(solution)/shard_map/ppermute | solution.py:13
  79.9 2.6 collective-permute-done.3
  83.3 1.4 convolution_bitcast_fusion.12
  85.2 6.1 %collective-permute-start.4 = (bf16[512,256]{1,0:T(8,128)(2,1)S(1)}, bf16[512,256]{1,0:T(8,128)(2,1)S(1)}, u32[]{:S(2)}, u32[]{:S(2)}) collective-permute-start(bf16[512,256]{1,0:T(8,128)(2,1)S(1)} %copy-done.4), channel_id=1, source_target_pairs={{0,30},{2,0},{4,2},{6,4},{8,6},{10,8},{12,10},{14,12},{16,14},{18,... | collective-permute-start | bytes 786440 | tf_op jit(solution)/shard_map/ppermute | solution.py:13
  92.6 2.6 collective-permute-done.4
  96.0 1.4 convolution_bitcast_fusion.11
  97.9 6.1 %collective-permute-start.5 = (bf16[512,256]{1,0:T(8,128)(2,1)S(1)}, bf16[512,256]{1,0:T(8,128)(2,1)S(1)}, u32[]{:S(2)}, u32[]{:S(2)}) collective-permute-start(bf16[512,256]{1,0:T(8,128)(2,1)S(1)} %copy-done.6), channel_id=1, source_target_pairs={{0,30},{2,0},{4,2},{6,4},{8,6},{10,8},{12,10},{14,12},{16,14},{18,... | collective-permute-start | bytes 786440 | tf_op jit(solution)/shard_map/ppermute | solution.py:13
  105.2 2.7 collective-permute-done.5
  108.6 1.4 convolution_bitcast_fusion.10
  110.5 6.1 %collective-permute-start.6 = (bf16[512,256]{1,0:T(8,128)(2,1)S(1)}, bf16[512,256]{1,0:T(8,128)(2,1)S(1)}, u32[]{:S(2)}, u32[]{:S(2)}) collective-permute-start(bf16[512,256]{1,0:T(8,128)(2,1)S(1)} %copy-done.8), channel_id=1, source_target_pairs={{0,30},{2,0},{4,2},{6,4},{8,6},{10,8},{12,10},{14,12},{16,14},{18,... | collective-permute-start | bytes 786440 | tf_op jit(solution)/shard_map/ppermute | solution.py:13
  118.0 2.6 collective-permute-done.6
  121.3 1.4 convolution_bitcast_fusion.9
  123.2 6.3 %collective-permute-start.7 = (bf16[512,256]{1,0:T(8,128)(2,1)S(1)}, bf16[512,256]{1,0:T(8,128)(2,1)S(1)}, u32[]{:S(2)}, u32[]{:S(2)}) collective-permute-start(bf16[512,256]{1,0:T(8,128)(2,1)S(1)} %copy-done.10), channel_id=1, source_target_pairs={{0,30},{2,0},{4,2},{6,4},{8,6},{10,8},{12,10},{14,12},{16,14},{18,... | collective-permute-start | bytes 786440 | tf_op jit(solution)/shard_map/ppermute | solution.py:13
  130.8 2.6 collective-permute-done.7
  137.8 2.0 all_gather.10
  142.6 6.1 %all-gather.3.cloned.1.call-done = f32[2,512,256]{2,1,0:T(8,128)} async-done(((f32[1,512,256]{2,1,0:T(8,128)}), f32[2,512,256]{2,1,0:T(8,128)}) %all-gather.3.cloned.1.call-update) | async-done | bytes 1048592 | tf_op jit(solution)/shard_map/all_gather | solution.py:54
  151.7 2.7 collective-permute-start.8
  157.1 9.9 %collective-permute-done.8 = bf16[512,256]{1,0:T(8,128)(2,1)S(1)} collective-permute-done((bf16[512,256]{1,0:T(8,128)(2,1)S(1)}, bf16[512,256]{1,0:T(8,128)(2,1)S(1)}, u32[]{:S(2)}, u32[]{:S(2)}) %collective-permute-start.8) | collective-permute-done | bytes 262176 | tf_op jit(solution)/shard_map/ppermute | solution.py:13
  167.0 5.5 %collective-permute-start.9 = (bf16[512,256]{1,0:T(8,128)(2,1)S(1)}, bf16[512,256]{1,0:T(8,128)(2,1)}, u32[]{:S(2)}, u32[]{:S(2)}) collective-permute-start(bf16[512,256]{1,0:T(8,128)(2,1)S(1)} %broadcast_select_fusion), channel_id=1, source_target_pairs={{0,30},{2,0},{4,2},{6,4},{8,6},{10,8},{12,10},{14,12},{16,14},{18,... | collective-permute-start | bytes 786440 | tf_op jit(solution)/shard_map/ppermute | solution.py:13
  175.8 2.9 collective-permute-done.9
  178.7 1.7 gather_fusion.9
  182.2 6.3 %collective-permute-start.10 = (bf16[512,256]{1,0:T(8,128)(2,1)}, bf16[512,256]{1,0:T(8,128)(2,1)}, u32[]{:S(2)}, u32[]{:S(2)}) collective-permute-start(bf16[512,256]{1,0:T(8,128)(2,1)} %collective-permute-done.9), channel_id=1, source_target_pairs={{0,30},{2,0},{4,2},{6,4},{8,6},{10,8},{12,10},{14,12},{16,14},{18,... | collective-permute-start | bytes 786440 | tf_op jit(solution)/shard_map/ppermute | solution.py:13
  189.8 4.2 %collective-permute-done.10 = bf16[512,256]{1,0:T(8,128)(2,1)} collective-permute-done((bf16[512,256]{1,0:T(8,128)(2,1)}, bf16[512,256]{1,0:T(8,128)(2,1)}, u32[]{:S(2)}, u32[]{:S(2)}) %collective-permute-start.10) | collective-permute-done | bytes 262176 | tf_op jit(solution)/shard_map/ppermute | solution.py:13
  194.0 1.5 gather_fusion.10
  195.5 1.4 convolution_bitcast_fusion.5
  197.4 6.2 %collective-permute-start.11 = (bf16[512,256]{1,0:T(8,128)(2,1)}, bf16[512,256]{1,0:T(8,128)(2,1)}, u32[]{:S(2)}, u32[]{:S(2)}) collective-permute-start(bf16[512,256]{1,0:T(8,128)(2,1)} %collective-permute-done.10), channel_id=1, source_target_pairs={{0,30},{2,0},{4,2},{6,4},{8,6},{10,8},{12,10},{14,12},{16,14},{18,... | collective-permute-start | bytes 786440 | tf_op jit(solution)/shard_map/ppermute | solution.py:13
  204.9 3.1 collective-permute-done.11
  208.0 1.5 gather_fusion.11
  211.4 6.3 %collective-permute-start.12 = (bf16[512,256]{1,0:T(8,128)(2,1)}, bf16[512,256]{1,0:T(8,128)(2,1)}, u32[]{:S(2)}, u32[]{:S(2)}) collective-permute-start(bf16[512,256]{1,0:T(8,128)(2,1)} %collective-permute-done.11), channel_id=1, source_target_pairs={{0,30},{2,0},{4,2},{6,4},{8,6},{10,8},{12,10},{14,12},{16,14},{18,... | collective-permute-start | bytes 786440 | tf_op jit(solution)/shard_map/ppermute | solution.py:13
  218.3 3.6 %collective-permute-done.12 = bf16[512,256]{1,0:T(8,128)(2,1)} collective-permute-done((bf16[512,256]{1,0:T(8,128)(2,1)}, bf16[512,256]{1,0:T(8,128)(2,1)}, u32[]{:S(2)}, u32[]{:S(2)}) %collective-permute-start.12) | collective-permute-done | bytes 262176 | tf_op jit(solution)/shard_map/ppermute | solution.py:13
  221.9 1.5 gather_fusion.12
  225.3 6.1 %collective-permute-start.13 = (bf16[512,256]{1,0:T(8,128)(2,1)}, bf16[512,256]{1,0:T(8,128)(2,1)}, u32[]{:S(2)}, u32[]{:S(2)}) collective-permute-start(bf16[512,256]{1,0:T(8,128)(2,1)} %collective-permute-done.12), channel_id=1, source_target_pairs={{0,30},{2,0},{4,2},{6,4},{8,6},{10,8},{12,10},{14,12},{16,14},{18,... | collective-permute-start | bytes 786440 | tf_op jit(solution)/shard_map/ppermute | solution.py:13
  232.0 3.6 %collective-permute-done.13 = bf16[512,256]{1,0:T(8,128)(2,1)} collective-permute-done((bf16[512,256]{1,0:T(8,128)(2,1)}, bf16[512,256]{1,0:T(8,128)(2,1)}, u32[]{:S(2)}, u32[]{:S(2)}) %collective-permute-start.13) | collective-permute-done | bytes 262176 | tf_op jit(solution)/shard_map/ppermute | solution.py:13
  235.6 1.5 gather_fusion.13
  239.1 6.4 %collective-permute-start.14 = (bf16[512,256]{1,0:T(8,128)(2,1)}, bf16[512,256]{1,0:T(8,128)(2,1)}, u32[]{:S(2)}, u32[]{:S(2)}) collective-permute-start(bf16[512,256]{1,0:T(8,128)(2,1)} %collective-permute-done.13), channel_id=1, source_target_pairs={{0,30},{2,0},{4,2},{6,4},{8,6},{10,8},{12,10},{14,12},{16,14},{18,... | collective-permute-start | bytes 786440 | tf_op jit(solution)/shard_map/ppermute | solution.py:13
  246.0 3.6 %collective-permute-done.14 = bf16[512,256]{1,0:T(8,128)(2,1)} collective-permute-done((bf16[512,256]{1,0:T(8,128)(2,1)}, bf16[512,256]{1,0:T(8,128)(2,1)}, u32[]{:S(2)}, u32[]{:S(2)}) %collective-permute-start.14) | collective-permute-done | bytes 262176 | tf_op jit(solution)/shard_map/ppermute | solution.py:13
  249.7 1.6 gather_fusion.14
  253.2 6.2 %collective-permute-start.15 = (bf16[512,256]{1,0:T(8,128)(2,1)}, bf16[512,256]{1,0:T(8,128)(2,1)S(1)}, u32[]{:S(2)}, u32[]{:S(2)}) collective-permute-start(bf16[512,256]{1,0:T(8,128)(2,1)} %collective-permute-done.14), channel_id=1, source_target_pairs={{0,30},{2,0},{4,2},{6,4},{8,6},{10,8},{12,10},{14,12},{16,14},{18,... | collective-permute-start | bytes 786440 | tf_op jit(solution)/shard_map/ppermute | solution.py:13
  260.0 3.7 %collective-permute-done.15 = bf16[512,256]{1,0:T(8,128)(2,1)S(1)} collective-permute-done((bf16[512,256]{1,0:T(8,128)(2,1)}, bf16[512,256]{1,0:T(8,128)(2,1)S(1)}, u32[]{:S(2)}, u32[]{:S(2)}) %collective-permute-start.15) | collective-permute-done | bytes 262176 | tf_op jit(solution)/shard_map/ppermute | solution.py:13
  268.0 40.5 %psum.15 = f32[256]{0:T(256)S(1)} all-reduce(f32[256]{0:T(256)S(1)} %convert_reduce_fusion), channel_id=1, replica_groups=mesh['row'=16,'rep'=2] {'row','rep'}, use_global_device_ids=true, to_apply=%region_4.6 | all-reduce | flops 256 | bytes 2048 | tf_op jit(solution)/shard_map/psum | solution.py:100
  309.8 1.7 broadcast_multiply_fusion
  (241 shorter events, 93.3 us)
Async XLA Ops:
  7.2 142.9 %copy-start = (bf16[256,256]{1,0:T(8,128)(2,1)S(1)}, bf16[256,256]{1,0:T(8,128)(2,1)}, u32[]{:S(2)}) copy-start(bf16[256,256]{1,0:T(8,128)(2,1)} %param.13) | copy-start | bytes 393220
  7.2 141.6 %all-gather.3.cloned.1.call-start = ((), (), s32[]{:S(2)}) async-start(), calls=%async_computation | async-start | bytes 1572864 | tf_op jit(solution)/shard_map/all_gather | solution.py:54
  7.2 41.6 %collective-permute-start = (bf16[512,256]{1,0:T(8,128)(2,1)}, bf16[512,256]{1,0:T(8,128)(2,1)S(1)}, u32[]{:S(2)}, u32[]{:S(2)}) collective-permute-start(bf16[512,256]{1,0:T(8,128)(2,1)} %param.12), channel_id=1, source_target_pairs={{0,16},{2,18},{4,20},{6,22},{8,24},{10,26},{12,28},{14,30},{16,0},... | collective-permute-start | bytes 786440 | tf_op jit(solution)/shard_map/ppermute | solution.py:13
  32.5 20.6 %copy-start.24 = (s32[8,2]{0,1:T(2,128)}, s32[8,2]{0,1:T(2,128)S(1)}, u32[]{:S(2)}) copy-start(s32[8,2]{0,1:T(2,128)S(1)} %get-tuple-element.43) | copy-start | bytes 196
  32.5 20.6 %copy-start.26 = (s32[8,2]{0,1:T(2,128)}, s32[8,2]{0,1:T(2,128)S(1)}, u32[]{:S(2)}) copy-start(s32[8,2]{0,1:T(2,128)S(1)} %get-tuple-element.44) | copy-start | bytes 196
  32.5 20.6 %copy-start.28 = (s32[8,2]{0,1:T(2,128)}, s32[8,2]{0,1:T(2,128)S(1)}, u32[]{:S(2)}) copy-start(s32[8,2]{0,1:T(2,128)S(1)} %get-tuple-element.45) | copy-start | bytes 196
  32.5 23.0 %copy-start.14 = (s32[8,2]{0,1:T(2,128)}, s32[8,2]{0,1:T(2,128)S(1)}, u32[]{:S(2)}) copy-start(s32[8,2]{0,1:T(2,128)S(1)} %get-tuple-element.39) | copy-start | bytes 196
  32.5 23.0 %copy-start.16 = (s32[8,2]{0,1:T(2,128)}, s32[8,2]{0,1:T(2,128)S(1)}, u32[]{:S(2)}) copy-start(s32[8,2]{0,1:T(2,128)S(1)} %get-tuple-element.46) | copy-start | bytes 196
  32.5 23.0 %copy-start.18 = (s32[8,2]{0,1:T(2,128)}, s32[8,2]{0,1:T(2,128)S(1)}, u32[]{:S(2)}) copy-start(s32[8,2]{0,1:T(2,128)S(1)} %get-tuple-element.40) | copy-start | bytes 196
  32.5 23.0 %copy-start.20 = (s32[8,2]{0,1:T(2,128)}, s32[8,2]{0,1:T(2,128)S(1)}, u32[]{:S(2)}) copy-start(s32[8,2]{0,1:T(2,128)S(1)} %get-tuple-element.41) | copy-start | bytes 196
  32.5 23.0 %copy-start.22 = (s32[8,2]{0,1:T(2,128)}, s32[8,2]{0,1:T(2,128)S(1)}, u32[]{:S(2)}) copy-start(s32[8,2]{0,1:T(2,128)S(1)} %get-tuple-element.42) | copy-start | bytes 196
  49.8 7.6 %collective-permute-start.1 = (bf16[512,256]{1,0:T(8,128)(2,1)S(1)}, bf16[512,256]{1,0:T(8,128)(2,1)S(1)}, u32[]{:S(2)}, u32[]{:S(2)}) collective-permute-start(bf16[512,256]{1,0:T(8,128)(2,1)S(1)} %broadcast_select_fusion.1), channel_id=1, source_target_pairs={{0,30},{2,0},{4,2},{6,4},{8,6},{10,8},{12,10},{14,12},{16,14},{18,... | collective-permute-start | bytes 786440 | tf_op jit(solution)/shard_map/ppermute | solution.py:13
  59.9 10.0 %collective-permute-start.2 = (bf16[512,256]{1,0:T(8,128)(2,1)S(1)}, bf16[512,256]{1,0:T(8,128)(2,1)S(1)}, u32[]{:S(2)}, u32[]{:S(2)}) collective-permute-start(bf16[512,256]{1,0:T(8,128)(2,1)S(1)} %collective-permute-done.1), channel_id=1, source_target_pairs={{0,30},{2,0},{4,2},{6,4},{8,6},{10,8},{12,10},{14,12},{16,14},{18,... | collective-permute-start | bytes 786440 | tf_op jit(solution)/shard_map/ppermute | solution.py:13
  72.5 10.0 %collective-permute-start.3 = (bf16[512,256]{1,0:T(8,128)(2,1)S(1)}, bf16[512,256]{1,0:T(8,128)(2,1)S(1)}, u32[]{:S(2)}, u32[]{:S(2)}) collective-permute-start(bf16[512,256]{1,0:T(8,128)(2,1)S(1)} %copy-done.2), channel_id=1, source_target_pairs={{0,30},{2,0},{4,2},{6,4},{8,6},{10,8},{12,10},{14,12},{16,14},{18,... | collective-permute-start | bytes 786440 | tf_op jit(solution)/shard_map/ppermute | solution.py:13
  85.2 10.0 %collective-permute-start.4 = (bf16[512,256]{1,0:T(8,128)(2,1)S(1)}, bf16[512,256]{1,0:T(8,128)(2,1)S(1)}, u32[]{:S(2)}, u32[]{:S(2)}) collective-permute-start(bf16[512,256]{1,0:T(8,128)(2,1)S(1)} %copy-done.4), channel_id=1, source_target_pairs={{0,30},{2,0},{4,2},{6,4},{8,6},{10,8},{12,10},{14,12},{16,14},{18,... | collective-permute-start | bytes 786440 | tf_op jit(solution)/shard_map/ppermute | solution.py:13
  97.9 10.0 %collective-permute-start.5 = (bf16[512,256]{1,0:T(8,128)(2,1)S(1)}, bf16[512,256]{1,0:T(8,128)(2,1)S(1)}, u32[]{:S(2)}, u32[]{:S(2)}) collective-permute-start(bf16[512,256]{1,0:T(8,128)(2,1)S(1)} %copy-done.6), channel_id=1, source_target_pairs={{0,30},{2,0},{4,2},{6,4},{8,6},{10,8},{12,10},{14,12},{16,14},{18,... | collective-permute-start | bytes 786440 | tf_op jit(solution)/shard_map/ppermute | solution.py:13
  110.5 10.0 %collective-permute-start.6 = (bf16[512,256]{1,0:T(8,128)(2,1)S(1)}, bf16[512,256]{1,0:T(8,128)(2,1)S(1)}, u32[]{:S(2)}, u32[]{:S(2)}) collective-permute-start(bf16[512,256]{1,0:T(8,128)(2,1)S(1)} %copy-done.8), channel_id=1, source_target_pairs={{0,30},{2,0},{4,2},{6,4},{8,6},{10,8},{12,10},{14,12},{16,14},{18,... | collective-permute-start | bytes 786440 | tf_op jit(solution)/shard_map/ppermute | solution.py:13
  123.2 10.9 %copy-start.50 = (pred[8]{0:T(512)(128)(4,1)S(1)}, pred[8]{0:T(512)(128)(4,1)}, u32[]{:S(2)}) copy-start(pred[8]{0:T(512)(128)(4,1)} %get-tuple-element.21) | copy-start | bytes 28
  123.2 10.2 %collective-permute-start.7 = (bf16[512,256]{1,0:T(8,128)(2,1)S(1)}, bf16[512,256]{1,0:T(8,128)(2,1)S(1)}, u32[]{:S(2)}, u32[]{:S(2)}) collective-permute-start(bf16[512,256]{1,0:T(8,128)(2,1)S(1)} %copy-done.10), channel_id=1, source_target_pairs={{0,30},{2,0},{4,2},{6,4},{8,6},{10,8},{12,10},{14,12},{16,14},{18,... | collective-permute-start | bytes 786440 | tf_op jit(solution)/shard_map/ppermute | solution.py:13
  136.1 6.0 %copy-start.15 = (s32[8,2]{0,1:T(2,128)S(1)}, s32[8,2]{0,1:T(2,128)}, u32[]{:S(2)}) copy-start(s32[8,2]{0,1:T(2,128)} %copy-done.14) | copy-start | bytes 196
  136.1 5.9 %copy-start.17 = (s32[8,2]{0,1:T(2,128)S(1)}, s32[8,2]{0,1:T(2,128)}, u32[]{:S(2)}) copy-start(s32[8,2]{0,1:T(2,128)} %copy-done.16) | copy-start | bytes 196
  136.8 13.3 %copy-start.53 = (f32[256]{0:T(256)S(1)}, f32[256]{0:T(256)}, u32[]{:S(2)}) copy-start(f32[256]{0:T(256)} %param.14) | copy-start | bytes 3076
  137.7 172.1 %all-reduce.2.cloned.1.call-start = ((), (), s32[]{:S(2)}) async-start(), calls=%async_computation.2 | async-start | bytes 524288 | tf_op jit(solution)/shard_map/psum | solution.py:100
  150.1 5.4 %copy-start.38 = (s32[8]{0:T(128)S(1)}, s32[8]{0:T(128)}, u32[]{:S(2)}) copy-start(s32[8]{0:T(128)} %get-tuple-element.6) | copy-start | bytes 100
  151.4 21.8 %copy-start.47 = (pred[8]{0:T(512)(128)(4,1)S(1)}, pred[8]{0:T(512)(128)(4,1)}, u32[]{:S(2)}) copy-start(pred[8]{0:T(512)(128)(4,1)} %get-tuple-element.19) | copy-start | bytes 28
  151.7 15.3 %collective-permute-start.8 = (bf16[512,256]{1,0:T(8,128)(2,1)S(1)}, bf16[512,256]{1,0:T(8,128)(2,1)S(1)}, u32[]{:S(2)}, u32[]{:S(2)}) collective-permute-start(bf16[512,256]{1,0:T(8,128)(2,1)S(1)} %convolution_convert_fusion), channel_id=1, source_target_pairs={{0,16},{2,18},{4,20},{6,22},{8,24},{10,26},{12,28},{14,30},{16,0},... | collective-permute-start | bytes 786440 | tf_op jit(solution)/shard_map/ppermute | solution.py:13
  157.1 154.4 %all-gather.5.cloned.1.call-start = ((), (), s32[]{:S(2)}) async-start(), calls=%async_computation.1 | async-start | bytes 1572864 | tf_op jit(solution)/shard_map/all_gather | solution.py:54
  167.0 11.6 %collective-permute-start.9 = (bf16[512,256]{1,0:T(8,128)(2,1)S(1)}, bf16[512,256]{1,0:T(8,128)(2,1)}, u32[]{:S(2)}, u32[]{:S(2)}) collective-permute-start(bf16[512,256]{1,0:T(8,128)(2,1)S(1)} %broadcast_select_fusion), channel_id=1, source_target_pairs={{0,30},{2,0},{4,2},{6,4},{8,6},{10,8},{12,10},{14,12},{16,14},{18,... | collective-permute-start | bytes 786440 | tf_op jit(solution)/shard_map/ppermute | solution.py:13
  182.2 11.8 %collective-permute-start.10 = (bf16[512,256]{1,0:T(8,128)(2,1)}, bf16[512,256]{1,0:T(8,128)(2,1)}, u32[]{:S(2)}, u32[]{:S(2)}) collective-permute-start(bf16[512,256]{1,0:T(8,128)(2,1)} %collective-permute-done.9), channel_id=1, source_target_pairs={{0,30},{2,0},{4,2},{6,4},{8,6},{10,8},{12,10},{14,12},{16,14},{18,... | collective-permute-start | bytes 786440 | tf_op jit(solution)/shard_map/ppermute | solution.py:13
  195.5 8.1 %copy-start.36 = (s32[8]{0:T(128)S(1)}, s32[8]{0:T(128)}, u32[]{:S(2)}) copy-start(s32[8]{0:T(128)} %get-tuple-element.85) | copy-start | bytes 100
  197.4 10.6 %collective-permute-start.11 = (bf16[512,256]{1,0:T(8,128)(2,1)}, bf16[512,256]{1,0:T(8,128)(2,1)}, u32[]{:S(2)}, u32[]{:S(2)}) collective-permute-start(bf16[512,256]{1,0:T(8,128)(2,1)} %collective-permute-done.10), channel_id=1, source_target_pairs={{0,30},{2,0},{4,2},{6,4},{8,6},{10,8},{12,10},{14,12},{16,14},{18,... | collective-permute-start | bytes 786440 | tf_op jit(solution)/shard_map/ppermute | solution.py:13
  209.5 8.2 %copy-start.35 = (s32[8]{0:T(128)S(1)}, s32[8]{0:T(128)}, u32[]{:S(2)}) copy-start(s32[8]{0:T(128)} %get-tuple-element.84) | copy-start | bytes 100
  209.5 8.2 %copy-start.46 = (pred[8]{0:T(512)(128)(4,1)S(1)}, pred[8]{0:T(512)(128)(4,1)}, u32[]{:S(2)}) copy-start(pred[8]{0:T(512)(128)(4,1)} %iota_compare_fusion.20) | copy-start | bytes 28
  211.4 10.5 %collective-permute-start.12 = (bf16[512,256]{1,0:T(8,128)(2,1)}, bf16[512,256]{1,0:T(8,128)(2,1)}, u32[]{:S(2)}, u32[]{:S(2)}) collective-permute-start(bf16[512,256]{1,0:T(8,128)(2,1)} %collective-permute-done.11), channel_id=1, source_target_pairs={{0,30},{2,0},{4,2},{6,4},{8,6},{10,8},{12,10},{14,12},{16,14},{18,... | collective-permute-start | bytes 786440 | tf_op jit(solution)/shard_map/ppermute | solution.py:13
  223.4 8.0 %copy-start.34 = (s32[8]{0:T(128)S(1)}, s32[8]{0:T(128)}, u32[]{:S(2)}) copy-start(s32[8]{0:T(128)} %get-tuple-element.83) | copy-start | bytes 100
  223.4 8.0 %copy-start.45 = (pred[8]{0:T(512)(128)(4,1)S(1)}, pred[8]{0:T(512)(128)(4,1)}, u32[]{:S(2)}) copy-start(pred[8]{0:T(512)(128)(4,1)} %iota_compare_fusion.19) | copy-start | bytes 28
  225.3 11.9 %copy-start.44 = (pred[8]{0:T(512)(128)(4,1)S(1)}, pred[8]{0:T(512)(128)(4,1)}, u32[]{:S(2)}) copy-start(pred[8]{0:T(512)(128)(4,1)} %get-tuple-element.9) | copy-start | bytes 28
  225.3 10.3 %collective-permute-start.13 = (bf16[512,256]{1,0:T(8,128)(2,1)}, bf16[512,256]{1,0:T(8,128)(2,1)}, u32[]{:S(2)}, u32[]{:S(2)}) collective-permute-start(bf16[512,256]{1,0:T(8,128)(2,1)} %collective-permute-done.12), channel_id=1, source_target_pairs={{0,30},{2,0},{4,2},{6,4},{8,6},{10,8},{12,10},{14,12},{16,14},{18,... | collective-permute-start | bytes 786440 | tf_op jit(solution)/shard_map/ppermute | solution.py:13
  237.2 8.3 %copy-start.32 = (s32[8]{0:T(128)S(1)}, s32[8]{0:T(128)}, u32[]{:S(2)}) copy-start(s32[8]{0:T(128)} %get-tuple-element.82) | copy-start | bytes 100
  237.2 8.2 %copy-start.43 = (pred[8]{0:T(512)(128)(4,1)S(1)}, pred[8]{0:T(512)(128)(4,1)}, u32[]{:S(2)}) copy-start(pred[8]{0:T(512)(128)(4,1)} %iota_compare_fusion.18) | copy-start | bytes 28
  239.1 12.3 %copy-start.42 = (pred[8]{0:T(512)(128)(4,1)S(1)}, pred[8]{0:T(512)(128)(4,1)}, u32[]{:S(2)}) copy-start(pred[8]{0:T(512)(128)(4,1)} %get-tuple-element.7) | copy-start | bytes 28
  239.1 10.6 %collective-permute-start.14 = (bf16[512,256]{1,0:T(8,128)(2,1)}, bf16[512,256]{1,0:T(8,128)(2,1)}, u32[]{:S(2)}, u32[]{:S(2)}) collective-permute-start(bf16[512,256]{1,0:T(8,128)(2,1)} %collective-permute-done.13), channel_id=1, source_target_pairs={{0,30},{2,0},{4,2},{6,4},{8,6},{10,8},{12,10},{14,12},{16,14},{18,... | collective-permute-start | bytes 786440 | tf_op jit(solution)/shard_map/ppermute | solution.py:13
  251.3 8.1 %copy-start.31 = (s32[8]{0:T(128)S(1)}, s32[8]{0:T(128)}, u32[]{:S(2)}) copy-start(s32[8]{0:T(128)} %get-tuple-element.81) | copy-start | bytes 100
  251.4 8.1 %copy-start.41 = (pred[8]{0:T(512)(128)(4,1)S(1)}, pred[8]{0:T(512)(128)(4,1)}, u32[]{:S(2)}) copy-start(pred[8]{0:T(512)(128)(4,1)} %iota_compare_fusion.17) | copy-start | bytes 28
  253.2 11.3 %copy-start.40 = (pred[8]{0:T(512)(128)(4,1)S(1)}, pred[8]{0:T(512)(128)(4,1)}, u32[]{:S(2)}) copy-start(pred[8]{0:T(512)(128)(4,1)} %get-tuple-element.5) | copy-start | bytes 28
  253.2 10.5 %collective-permute-start.15 = (bf16[512,256]{1,0:T(8,128)(2,1)}, bf16[512,256]{1,0:T(8,128)(2,1)S(1)}, u32[]{:S(2)}, u32[]{:S(2)}) collective-permute-start(bf16[512,256]{1,0:T(8,128)(2,1)} %collective-permute-done.14), channel_id=1, source_target_pairs={{0,30},{2,0},{4,2},{6,4},{8,6},{10,8},{12,10},{14,12},{16,14},{18,... | collective-permute-start | bytes 786440 | tf_op jit(solution)/shard_map/ppermute | solution.py:13
  266.4 42.2 %copy-start.12 = (f32[512,256]{1,0:T(8,128)S(1)}, f32[512,256]{1,0:T(8,128)}, u32[]{:S(2)}) copy-start(f32[512,256]{1,0:T(8,128)} %get-tuple-element.38) | copy-start | bytes 1572868
  266.4 42.1 %copy-start.13 = (f32[512,256]{1,0:T(8,128)S(1)}, f32[512,256]{1,0:T(8,128)}, u32[]{:S(2)}) copy-start(f32[512,256]{1,0:T(8,128)} %get-tuple-element.71) | copy-start | bytes 1572868
  (25 other events, 65.0 us)
Sparse Core Ops, SparseCore 0:
  137.8 10.8 all-gather.2
  157.2 124.5 all-reduce.1
  283.3 8.0 all-gather.4
